TPU v7x, 768 devices: a whole 4x8x12 slice. The times are simulated.
768 devices in a mesh: aux: 12 (over z), pair: 64 (over x, y, core).
Axes of the slice: x: 4, y: 8, z: 12, core: 2. Of those that a mesh axis runs over, the one named last changes fastest.
Arguments:
- integrals: bfloat16 [1152, 393216], P('aux', 'pair'), may hold values from -6 to 6
- tile_mask: int32 [12, 6144], P('aux', 'pair'), may hold values 0 or 1
- metric: bfloat16 [1152, 1152], P('pair'), may hold values from -0.0048828125 to 0.0048828125
- owners: int32 [6144], P('pair'), may hold values from 0 to 767
Outputs:
- owner_sums: float32 [768, 64], P(('aux', 'pair'))
Inputs may be any that keep to these rules, and one draw needn't show every extreme that they name: `owners`: a device is numbered aux index times 64 plus pair index.
All inputs are finite; a program needn't handle non-finite values. No bound on the sum of `tile_mask` on one device may be relied on, other than what follows from the above.
Results may differ from a plain program's by a relative error of at most 0.0003.
Values may be sent and summed in bfloat16 or wider, within the bound.
A program may use at most 32 MiB of HBM per device.

v0:
```python
import jax
import jax.numpy as jnp
from jax import lax
from jax.sharding import PartitionSpec as P

TILE = 64


def body(integrals, tile_mask, metric, owners):
    aux_rows = integrals.shape[0]
    groups = lax.axis_size("aux")
    pairs_count = lax.axis_size("pair")
    tiles_here = tile_mask.shape[1]
    per_group = tiles_here // groups
    keep = tile_mask.reshape(1, groups, per_group, 1).astype(jnp.bfloat16)
    blocks = integrals.reshape(aux_rows, groups, per_group, TILE) * keep
    moved = lax.all_to_all(blocks, "aux", split_axis=1, concat_axis=0, tiled=True)
    flat = moved.reshape(moved.shape[0], per_group * TILE)
    image = jnp.dot(
        lax.all_gather(metric, "pair", axis=0, tiled=True), flat, preferred_element_type=jnp.float32
    )
    summed = jnp.sum(flat.astype(jnp.float32) * image, axis=0)
    weights = summed.reshape(per_group, TILE)
    mine = lax.dynamic_slice_in_dim(owners, lax.axis_index("aux") * per_group, per_group, 0)
    myself = lax.axis_index("aux") * pairs_count + lax.axis_index("pair")
    values = lax.all_gather(weights, ("aux", "pair"), axis=0, tiled=True)
    owner_ids = lax.all_gather(mine, ("aux", "pair"), axis=0, tiled=True)
    hits = (owner_ids == myself).astype(jnp.float32)
    return jnp.dot(hits[None, :], values, precision=lax.Precision.HIGHEST)


def solution(mesh):
    return jax.shard_map(
        body,
        mesh=mesh,
        in_specs=(P("aux", "pair"), P("aux", "pair"), P("pair", None), P("pair")),
        out_specs=P(("aux", "pair"), None),
        check_vma=False,
    )
```

profile of v0, /device:TPU:1, one launch (start us, length us, event | category | flops | bytes accessed | tf_op | source)
XLA Modules:
  0.0 291.1 jit_solution(2047303396569390067)
XLA Ops:
  6.5 0.0 all-gather.6.cloned.1.call-start
  6.5 0.7 all-gather.6.cloned.1.call-update
  7.3 0.0 all-gather.4.cloned.1.call-start
  7.3 0.7 convert_reduce_fusion
  8.0 0.1 convert_element_type.16
  8.1 1.9 copy.16
  9.9 0.2 broadcast_multiply_fusion
  10.1 72.1 %all_to_all.15 = bf16[96,12,8,64]{0,3,2,1:T(8,128)(2,1)S(1)} all-to-all(bf16[96,12,8,64]{0,3,2,1:T(8,128)(2,1)S(1)} %broadcast_multiply_fusion), channel_id=1, replica_groups=mesh['aux'=12,'pair'=64] {'aux'}, dimensions={1} | all-to-all | bytes 2359296 | tf_op jit(solution)/shard_map/all_to_all | solution.py:17
  82.2 1.1 copy.17
  83.3 2.7 reshape.23
  86.1 22.5 %all-gather.6.cloned.1.call-done = bf16[64,18,1152]{2,1,0:T(8,128)(2,1)} async-done(((bf16[1,18,1152]{2,1,0:T(8,128)(2,1)}), bf16[64,18,1152]{2,1,0:T(8,128)(2,1)}) %all-gather.6.cloned.1.call-update) | async-done | bytes 2654224 | tf_op jit(solution)/shard_map/all_gather | solution.py:20
  108.6 3.9 %reshape.28 = bf16[1152,1152]{1,0:T(8,128)(2,1)S(1)} reshape(bf16[64,18,1152]{2,1,0:T(8,128)(2,1)} %all-gather.6.cloned.1.call-done) | data formatting | bytes 5308416
  112.4 0.0 copy-start
  112.5 3.6 %fusion.1 = f32[512]{0:T(512)S(1)} fusion(bf16[1152,512]{0,1:T(8,128)(2,1)} %reshape.23, bf16[1152,1152]{1,0:T(8,128)(2,1)S(1)} %reshape.28), kind=kOutput, calls=%fused_computation.2 | convolution fusion | flops 1360723456 | bytes 3835904 | tf_op jit(solution)/shard_map/dot_general | solution.py:19
  116.0 0.7 reshape.24
  116.7 0.0 all-gather.4.cloned.1.call-update
  116.8 0.0 copy-done
  116.8 0.2 dynamic-slice_dynamic-update-slice_fusion
  117.0 110.1 %all-reduce = s32[6144]{0:T(1024)S(1)} all-reduce(s32[6144]{0:T(1024)S(1)} %dynamic-slice_dynamic-update-slice_fusion), channel_id=1, replica_groups=mesh['aux'=12,'pair'=64] {'aux','pair'}, use_global_device_ids=true, to_apply=%add | all-reduce | flops 6144 | bytes 49152
  227.1 53.7 %all-gather.4.cloned.1.call-done = f32[6144,64]{1,0:T(8,128)} async-done(((f32[8,64]{1,0:T(8,128)}), f32[6144,64]{1,0:T(8,128)}) %all-gather.4.cloned.1.call-update) | async-done | bytes 1572880 | tf_op jit(solution)/shard_map/all_gather | solution.py:26
  280.8 3.5 %fusion.2 = f32[1,64]{1,0:T(1,128)} fusion(pred[6144,1]{0,1:T(4,128)(4,1)S(1)} %reshape.29, f32[6144,64]{1,0:T(8,128)} %all-gather.4.cloned.1.call-done), kind=kOutput, calls=%fused_computation.7 | convolution fusion | flops 4718592 | bytes 1579264 | tf_op jit(solution)/shard_map/dot_general | solution.py:29
  (3 shorter events, 0.0 us)
Async XLA Ops:
  6.5 102.0 %all-gather.6.cloned.1.call-start = ((), (), s32[]{:S(2)}) async-start(), calls=%async_computation.2 | async-start | bytes 3594240 | tf_op jit(solution)/shard_map/all_gather | solution.py:20
  7.3 273.5 %all-gather.4.cloned.1.call-start = ((), (), s32[]{:S(2)}) async-start(), calls=%async_computation.1 | async-start | bytes 3149824 | tf_op jit(solution)/shard_map/all_gather | solution.py:26
  112.4 4.3 %copy-start = (s32[96]{0:T(128)S(1)}, s32[96]{0:T(128)}, u32[]{:S(2)}) copy-start(s32[96]{0:T(128)} %param.7) | copy-start | bytes 1156
Sparse Core Ops, SparseCore 0:
  11.3 97.2 all-gather.5
  116.9 163.8 all-gather.3
where the time goes:
time: 291 us
  blocking collectives  182 us (63%)
  waiting for transfers between devices  76.9 us (26%)
  between operations  13.5 us (5%)
  local copies, waits for them, and re-layouts  10.6 us (4%)
  matrix products  7.12 us (2%)
    unnamed x1, blocking collectives  110 us
    all_to_all x1, blocking collectives, body(): lax.all_to_all(blocks, 'aux', split_axis=1, concat_axis=0, tiled=True)  72.1 us
    all_gather x1, waiting for transfers between devices, body(): values = lax.all_gather(weights, ('aux', 'pair'), axis=0, tiled=True)  53.7 us
    all_gather x1, waiting for transfers between devices, body(): lax.all_gather(metric, 'pair', axis=0, tiled=True)  22.5 us
    unnamed x6, local copies, waits for them, and re-layouts  5.94 us
  transfers between devices with their start and end apart: 2, of which 2 were waited for; matrix products, arithmetic and copies ran while one was open for 2% of the time, Pallas kernels for 0%

commit v1 on v0

v1 whole, which is shorter than its diff:
```python
import functools

import jax
import jax.numpy as jnp
from jax import lax
from jax.experimental import pallas as pl
from jax.experimental.pallas import tpu as pltpu
from jax.sharding import PartitionSpec as P

MESH = pl.DeviceIdType.MESH
F32, BF16, I32 = jnp.float32, jnp.bfloat16, jnp.int32
NZ, NX, NY = 12, 4, 8
AUXD, WIDTH, NAUX = 96, 512, 1152
CHUNKS = 2
CW = WIDTH // CHUNKS
LANES = 128
SHARD = 18
MAIN = 16
PACKED = NAUX + 2 * LANES
QB = 192
ORDER = (6, 5, 7, 4, 8, 3, 9, 2, 10, 1, 11)


def iota(shape, axis):
    return lax.broadcasted_iota(I32, shape, axis)


def kernel(
    x_hbm, mask_hbm, met_hbm, own_hbm, out_ref,
    src, got, mask, met, own, slots, dense, hits, terms, heard, part, got_y, fold, got_x,
    in_sem, z_send, z_recv, y_send, y_recv, x_send, x_recv, c_send, c_recv,
    t_send, t_recv, p_send, p_recv, q_send, q_recv,
):
    z = lax.axis_index("aux")
    pair = lax.axis_index("pair")
    c = lax.rem(pair, 2)
    y = lax.rem(pair // 2, NY)
    x = pair // (2 * NY)
    r = x * 2 + c

    def at_z(k):
        return lax.rem(z + k, NZ)

    def at_y(k):
        return lax.rem(y + k, NY)

    def at_r(k):
        return lax.rem(r + k, 2 * NX)

    def dev_z(k):
        return {"aux": at_z(k)}

    def dev_y(k):
        return {"pair": (x * NY + at_y(k)) * 2 + c}

    def dev_r(k):
        other = at_r(k)
        return {"pair": ((other // 2) * NY + y) * 2 + lax.rem(other, 2)}

    def dev_x(k):
        return {"pair": (lax.rem(x + k, NX) * NY + y) * 2 + c}

    dev_c = {"pair": (x * NY + y) * 2 + (1 - c)}

    barrier = pltpu.get_barrier_semaphore()
    peers = [dev_z(k) for k in range(1, NZ)] + [dev_y(k) for k in range(1, NY)] + [dev_r(k) for k in range(1, 2 * NX)]
    for peer in peers:
        pl.semaphore_signal(barrier, inc=1, device_id=peer, device_id_type=MESH)

    met_in = pltpu.make_async_copy(met_hbm, met, in_sem.at[NZ])
    mask_in = pltpu.make_async_copy(mask_hbm, mask, in_sem.at[NZ + 1])
    own_in = pltpu.make_async_copy(own_hbm, own, in_sem.at[NZ + 2])
    mask_in.start()
    met_in.start()
    loads = {}
    for k in ORDER + (0,):
        block = at_z(k)
        loads[k] = [
            pltpu.make_async_copy(
                x_hbm.at[:, pl.ds(pl.multiple_of(block * WIDTH + j * CW, LANES), CW)], src.at[block, j], in_sem.at[k]
            )
            for j in range(CHUNKS)
        ]
        for load in loads[k]:
            load.start()
    own_in.start()

    met_in.wait()
    rows = met[...].astype(F32)
    tail = rows[MAIN:SHARD]
    rest = jnp.concatenate([tail[:, i * LANES : (i + 1) * LANES] for i in range(8)], axis=0)
    last = jnp.concatenate([tail[:, 8 * LANES :], jnp.zeros((MAIN - 2, LANES), F32)], axis=0)
    slots[c, x, y] = jnp.concatenate([rows[:MAIN], rest, last], axis=1).astype(BF16)

    mask_in.wait()
    left_half = iota((1, LANES), 1) < 64

    def masked(k):
        block = at_z(k)
        for load in loads[k]:
            load.wait()
        for j in range(CHUNKS):
            for lane in range(CW // LANES):
                tile = block * 8 + (j * CW + lane * LANES) // 64
                keep = jnp.where(left_half, mask[0, tile], mask[0, tile + 1]).astype(F32).astype(BF16)
                cols = pl.ds(lane * LANES, LANES)
                if k == 0:
                    got[j, block, :, cols] = src[block, j, :, cols] * keep
                else:
                    src[block, j, :, cols] = src[block, j, :, cols] * keep

    for k in ORDER:
        masked(k)

    pl.semaphore_wait(barrier, len(peers))

    def remote(s, d, ss, rs, dev):
        return pltpu.make_async_remote_copy(src_ref=s, dst_ref=d, send_sem=ss, recv_sem=rs, device_id=dev, device_id_type=MESH)

    y_copies = [remote(slots.at[c, x, y], slots.at[c, x, y], y_send.at[k], y_recv.at[k], dev_y(k)) for k in range(1, NY)]
    for copy in y_copies:
        copy.start()
    z_copies = [
        [remote(src.at[at_z(k), j], got.at[j, z], z_send.at[j, k], z_recv.at[j, k], dev_z(k)) for k in ORDER]
        for j in range(CHUNKS)
    ]
    for group in z_copies:
        for copy in group:
            copy.start()
    masked(0)

    own_in.wait()
    s = iota((64, 96), 0)
    target = z * 64 + (((s & 7) >> 1) * NY + (s >> 3)) * 2 + (s & 1)
    hit = jnp.where(own[...] == target, 1.0, 0.0).astype(BF16)
    q = iota((96, 96), 1)
    t = iota((96, 96), 0)
    for j in range(CHUNKS):
        for par in range(2):
            wanted = (q >> 3) * 8 + 2 * (j * (CW // LANES) + (q & 7)) + par
            perm = jnp.where((t == wanted) & ((q & 7) < CW // LANES), 1.0, 0.0).astype(BF16)
            hits[j, pl.ds(par * 64, 64), :] = jnp.dot(hit, perm, preferred_element_type=F32).astype(BF16)

    def from_y(k):
        there = lax.rem(y + NY - k, NY)
        return remote(slots.at[c, x, there], slots.at[c, x, there], y_send.at[k], y_recv.at[k], dev_y(k))

    for k in range(1, NY):
        from_y(k).wait_recv()
    x_copies = [remote(slots.at[c, x], slots.at[c, x], x_send.at[k], x_recv.at[k], dev_x(k)) for k in range(1, NX)]
    for copy in x_copies:
        copy.start()
    for k in range(1, NX):
        there = lax.rem(x + NX - k, NX)
        remote(slots.at[c, there], slots.at[c, there], x_send.at[k], x_recv.at[k], dev_x(k)).wait_recv()
    c_copy = remote(slots.at[c], slots.at[c], c_send, c_recv, dev_c)
    c_copy.start()
    remote(slots.at[1 - c], slots.at[1 - c], c_send, c_recv, dev_c).wait_recv()

    def picks(index):
        row = iota((288, 256), 0)
        col = iota((288, 256), 1)
        yy = jnp.zeros_like(row)
        for step in range(1, NY):
            yy = yy + (row >= 36 * step).astype(I32)
        row = row - 36 * yy
        cc = (row >= SHARD).astype(I32)
        row = row - SHARD * cc
        base = cc * 128 + yy * MAIN
        if index is None:
            return jnp.where((row < MAIN) & (col == base + row), 1.0, 0.0).astype(BF16)
        return jnp.where((row >= MAIN) & (col == base + 2 * index + row - MAIN), 1.0, 0.0).astype(BF16)

    main_pick = picks(None)
    for piece in range(9):
        rest_pick = picks(piece % 8)
        cols = pl.ds(piece * LANES, LANES)
        rest_cols = pl.ds(NAUX + (piece // 8) * LANES, LANES)

        @pl.loop(0, NX)
        def _(xx):
            main = slots[:, xx, :, :, cols].reshape(256, LANES)
            extra = slots[:, xx, :, :, rest_cols].reshape(256, LANES)
            both = jnp.dot(main_pick, main, preferred_element_type=F32) + jnp.dot(rest_pick, extra, preferred_element_type=F32)
            dense[pl.ds(pl.multiple_of(xx * 288, 32), 288), cols] = both.astype(BF16)

    def chunk(j):
        for k in ORDER:
            there = lax.rem(z + NZ - k, NZ)
            remote(src.at[there, j], got.at[j, there], z_send.at[j, k], z_recv.at[j, k], dev_z(k)).wait_recv()
        block = got[j].reshape(NAUX, CW)
        acc = jnp.zeros((1, CW), F32)
        for i in range(NAUX // QB):
            image = jnp.dot(dense[pl.ds(i * QB, QB), :], block, preferred_element_type=F32)
            acc = acc + jnp.sum(block[i * QB : (i + 1) * QB].astype(F32) * image, axis=0, keepdims=True)
        pieces = [acc[:, i * LANES : (i + 1) * LANES] for i in range(CW // LANES)]
        terms[j] = jnp.concatenate(pieces + [jnp.zeros((8 - len(pieces), LANES), F32)], axis=0)
        heard[j, z] = terms[j]
        copies = [remote(terms.at[j], heard.at[j, z], t_send.at[j, k], t_recv.at[j, k], dev_z(k)) for k in range(1, NZ)]
        for copy in copies:
            copy.start()
        return copies

    def owned(j):
        for k in range(1, NZ):
            there = lax.rem(z + NZ - k, NZ)
            remote(terms.at[j], heard.at[j, there], t_send.at[j, k], t_recv.at[j, k], dev_z(k)).wait_recv()
        value = heard[j].reshape(96, LANES)
        first = value.astype(BF16)
        value = value - first.astype(F32)
        second = value.astype(BF16)
        third = (value - second.astype(F32)).astype(BF16)
        sums = [jnp.dot(hits[j], v, preferred_element_type=F32) for v in (third, second, first)]
        both = sums[0] + sums[1] + sums[2]
        return both[:64, :64] + both[64:, 64:]

    t_copies = [chunk(0)]
    total = None
    for j in range(1, CHUNKS):
        t_copies.append(chunk(j))
        mine = owned(j - 1)
        total = mine if total is None else total + mine
    mine = owned(CHUNKS - 1)
    total = mine if total is None else total + mine

    part[:, :, :64] = total.reshape(NY, 8, 64)
    part[:, :, 64:] = jnp.zeros((NY, 8, 64), F32)
    p_copies = [remote(part.at[at_y(k)], got_y.at[y], p_send.at[k], p_recv.at[k], dev_y(k)) for k in range(1, NY)]
    for copy in p_copies:
        copy.start()
    got_y[y] = part[y]
    for k in range(1, NY):
        there = lax.rem(y + NY - k, NY)
        remote(part.at[there], got_y.at[there], p_send.at[k], p_recv.at[k], dev_y(k)).wait_recv()
    fold[...] = jnp.sum(got_y[...], axis=0)
    q_copies = [remote(fold, got_x.at[r], q_send.at[k], q_recv.at[k], dev_r(k)) for k in range(1, 2 * NX)]
    for copy in q_copies:
        copy.start()
    got_x[r] = fold[...]
    for k in range(1, 2 * NX):
        there = lax.rem(r + 2 * NX - k, 2 * NX)
        remote(fold, got_x.at[there], q_send.at[k], q_recv.at[k], dev_r(k)).wait_recv()
    final = jnp.sum(got_x[...], axis=0)
    out_ref[...] = jnp.sum(jnp.where(iota((8, LANES), 0) == r, final, 0.0), axis=0, keepdims=True)[:, :64]

    for group in [y_copies, x_copies, [c_copy], p_copies, q_copies] + z_copies + t_copies:
        for copy in group:
            copy.wait_send()


def body(integrals, tile_mask, metric, owners):
    any_spec = pl.BlockSpec(memory_space=pl.ANY)
    dma = pltpu.SemaphoreType.DMA
    return pl.pallas_call(
        kernel,
        out_shape=jax.ShapeDtypeStruct((1, 64), F32),
        in_specs=[any_spec] * 4,
        out_specs=pl.BlockSpec(memory_space=pltpu.VMEM),
        scratch_shapes=[
            pltpu.VMEM((NZ, CHUNKS, AUXD, CW), BF16),
            pltpu.VMEM((CHUNKS, NZ, AUXD, CW), BF16),
            pltpu.SMEM((1, 96), I32),
            pltpu.VMEM((SHARD, NAUX), BF16),
            pltpu.VMEM((1, 96), I32),
            pltpu.VMEM((2, NX, NY, MAIN, PACKED), BF16),
            pltpu.VMEM((NAUX, NAUX), BF16),
            pltpu.VMEM((CHUNKS, 128, 96), BF16),
            pltpu.VMEM((CHUNKS, 8, LANES), F32),
            pltpu.VMEM((CHUNKS, NZ, 8, LANES), F32),
            pltpu.VMEM((NY, 8, LANES), F32),
            pltpu.VMEM((NY, 8, LANES), F32),
            pltpu.VMEM((8, LANES), F32),
            pltpu.VMEM((2 * NX, 8, LANES), F32),
            dma((NZ + 3,)),
            dma((CHUNKS, NZ)), dma((CHUNKS, NZ)),
            dma((NY,)), dma((NY,)),
            dma((NX,)), dma((NX,)),
            dma, dma,
            dma((CHUNKS, NZ)), dma((CHUNKS, NZ)),
            dma((NY,)), dma((NY,)),
            dma((2 * NX,)), dma((2 * NX,)),
        ],
        compiler_params=pltpu.CompilerParams(collective_id=0, has_side_effects=True, vmem_limit_bytes=40 << 20),
    )(integrals, tile_mask, metric, owners.reshape(1, -1))


def solution(mesh):
    return jax.shard_map(
        body,
        mesh=mesh,
        in_specs=(P("aux", "pair"), P("aux", "pair"), P("pair", None), P("pair")),
        out_specs=P(("aux", "pair"), None),
        check_vma=False,
    )
```

time: 291 us -> 82.2 us (0.28)
  blocking collectives: 182 us -> 0 us
  Pallas kernels: 0 us -> 78 us
  waiting for transfers between devices: 76.9 us -> 0 us
  between operations: 13.5 us -> 0.01 us
  matrix products: 7.12 us -> 0 us
  local copies, waits for them, and re-layouts: 10.6 us -> 3.91 us
    unnamed x1 -> x0, blocking collectives: 110 us -> none
    pallas_call x0 -> x1, Pallas kernels: none -> 78 us  [body(): pl.pallas_call(kernel, out_shape=jax.ShapeDtypeStruct((1, 64), F32), in_s...]
    all_gather x2 -> x0, waiting for transfers between devices: 76.1 us -> none  [the longest x1 53.7 us: body(): values = lax.all_gather(weights, ('aux', 'pair'), axis=0, tiled=True)]
    all_to_all x1 -> x0, blocking collectives: 72.1 us -> none  [body(): lax.all_to_all(blocks, 'aux', split_axis=1, concat_axis=0, tiled=True)]
    dot_general x2 -> x0, matrix products: 7.12 us -> none  [the longest x1 3.59 us: body(): jnp.dot(lax.all_gather(metric, 'pair', axis=0, tiled=True), flat, preferr...]
    reshape x2 -> x0, local copies, waits for them, and re-layouts: 3.42 us -> none  [the longest x1 2.74 us: body(): flat = moved.reshape(moved.shape[0], per_group * TILE)]
    unnamed x6 -> x9, local copies, waits for them, and re-layouts: 5.94 us -> 3.91 us
  transfers between devices with their start and end apart: 2 -> 0, of which waited for: 2 -> 0; matrix products, arithmetic and copies ran while one was open for 2% -> 0% of each run, Pallas kernels for 0% -> 0%
where the time goes in v1:
time: 82.2 us; the launch traced here: 81.9 us
  Pallas kernels  78 us (95%)
  local copies, waits for them, and re-layouts  3.91 us (5%)
    pallas_call x1, Pallas kernels, body(): pl.pallas_call(kernel, out_shape=jax.ShapeDtypeStruct((1, 64), F32), in_s...  78 us
    unnamed x9, local copies, waits for them, and re-layouts  3.91 us

profile of v1, /device:TPU:1, one launch (start us, length us, event | category | flops | bytes accessed | tf_op | source)
XLA Modules:
  0.0 81.9 jit_solution(959757938157981881)
XLA Ops:
  0.0 0.0 copy-start
  0.0 1.3 %copy-done = bf16[96,6144]{1,0:T(8,128)(2,1)S(1)} copy-done((bf16[96,6144]{1,0:T(8,128)(2,1)S(1)}, bf16[96,6144]{1,0:T(8,128)(2,1)}, u32[]{:S(2)}) %copy-start) | copy-done | bytes 1179672
  1.3 0.0 copy-start.1
  1.3 0.8 copy-done.1
  2.1 0.0 copy-start.2
  2.1 0.7 copy-done.2
  2.7 0.0 copy-start.3
  2.7 0.7 copy-done.3
  3.4 78.0 %shard_map.46 = f32[1,64]{1,0:T(1,128)S(1)} custom-call(bf16[96,6144]{1,0:T(8,128)(2,1)S(1)} %copy-done, s32[1,96]{1,0:T(1,128)S(1)} %copy-done.2, bf16[18,1152]{1,0:T(8,128)(2,1)S(1)} %copy-done.1, s32[1,96]{1,0:T(1,128)S(1)} %bitcast.1), custom_call_target="tpu_custom_call" | custom-call | tf_op jit(solution)/shard_map/pallas_call | solution.py:254
  81.4 0.5 copy.6
Async XLA Ops:
  0.0 1.3 %copy-start = (bf16[96,6144]{1,0:T(8,128)(2,1)S(1)}, bf16[96,6144]{1,0:T(8,128)(2,1)}, u32[]{:S(2)}) copy-start(bf16[96,6144]{1,0:T(8,128)(2,1)} %x_hbm.1) | copy-start | bytes 3538948
  1.3 0.8 copy-start.1
  2.1 0.7 copy-start.2
  2.7 0.7 copy-start.3

commit v2 on v0

v2 whole, which is shorter than its diff:
```python
import functools

import jax
import jax.numpy as jnp
from jax import lax
from jax.experimental import pallas as pl
from jax.experimental.pallas import tpu as pltpu
from jax.sharding import PartitionSpec as P

MESH = pl.DeviceIdType.MESH
F32, BF16, I32 = jnp.float32, jnp.bfloat16, jnp.int32
NZ, NX, NY = 12, 4, 8
AUXD, WIDTH, NAUX = 96, 512, 1152
CHUNKS = 2
CW = WIDTH // CHUNKS
LANES = 128
SHARD = 18
MAIN = 16
PACKED = NAUX + 2 * LANES
QB = 192
ORDER = (6, 5, 7, 4, 8, 3, 9, 2, 10, 1, 11)
AROUND = sorted(
    [(i, j) for i in range(NX) for j in range(NY) if i or j], key=lambda k: -min(k[0], NX - k[0]) - min(k[1], NY - k[1])
)


def iota(shape, axis):
    return lax.broadcasted_iota(I32, shape, axis)


def kernel(
    x_hbm, mask_hbm, met_hbm, own_hbm, out_ref,
    got, masks, keep, met, own, slots, dense, hits, terms, heard, part, rows_in,
    in_sem, z_send, z_recv, m_send, m_recv, o_send, o_recv, y_send, y_recv, x_send, x_recv, c_send, c_recv,
    t_send, t_recv, p_send, p_recv,
):
    z = lax.axis_index("aux")
    pair = lax.axis_index("pair")
    c = lax.rem(pair, 2)
    y = lax.rem(pair // 2, NY)
    x = pair // (2 * NY)
    place = x * NY + y

    def at_z(k):
        return lax.rem(z + k, NZ)

    def at_y(k):
        return lax.rem(y + k, NY)

    def dev_z(k):
        return {"aux": at_z(k)}

    def dev_zc(k, flip):
        return {"aux": at_z(k), "pair": place * 2 + (1 - c if flip else c)}

    def dev_y(k):
        return {"pair": (x * NY + at_y(k)) * 2 + c}

    def place_at(k):
        return lax.rem(x + k[0], NX) * NY + lax.rem(y + k[1], NY)

    def dev_xy(k):
        return {"pair": place_at(k) * 2 + c}

    def dev_x(k):
        return {"pair": (lax.rem(x + k, NX) * NY + y) * 2 + c}

    dev_c = {"pair": (x * NY + y) * 2 + (1 - c)}

    def remote(s, d, ss, rs, dev):
        return pltpu.make_async_remote_copy(src_ref=s, dst_ref=d, send_sem=ss, recv_sem=rs, device_id=dev, device_id_type=MESH)

    def columns(block, j):
        return x_hbm.at[:, pl.ds(pl.multiple_of(block * WIDTH + j * CW, LANES), CW)]

    met_in = pltpu.make_async_copy(met_hbm, met, in_sem.at[0])
    met_in.start()
    barrier = pltpu.get_barrier_semaphore()
    peers = [dev_zc(k, False) for k in ORDER] + [dev_xy(k) for k in AROUND] + [dev_zc(k, True) for k in ORDER + (0,)]
    for peer in peers:
        pl.semaphore_signal(barrier, inc=1, device_id=peer, device_id_type=MESH)
    locals_in = [
        pltpu.make_async_copy(mask_hbm, masks.at[z], in_sem.at[1]),
        pltpu.make_async_copy(own_hbm, own.at[c], in_sem.at[2]),
    ] + [pltpu.make_async_copy(columns(z, j), got.at[j, z], in_sem.at[3 + j]) for j in range(CHUNKS)]
    for copy in locals_in:
        copy.start()
    pl.semaphore_wait(barrier, len(peers))

    z_copies = [
        [remote(columns(at_z(k), j), got.at[j, z], z_send.at[j, k], z_recv.at[j, k], dev_z(k)) for k in ORDER]
        for j in range(CHUNKS)
    ]
    m_copies = [remote(mask_hbm, masks.at[z], m_send.at[k], m_recv.at[k], dev_z(k)) for k in ORDER]
    for copy in m_copies + z_copies[0]:
        copy.start()

    met_in.wait()
    rows = met[...].astype(F32)
    tail = rows[MAIN:SHARD]
    rest = jnp.concatenate([tail[:, i * LANES : (i + 1) * LANES] for i in range(8)], axis=0)
    last = jnp.concatenate([tail[:, 8 * LANES :], jnp.zeros((MAIN - 2, LANES), F32)], axis=0)
    slots[c, x, y] = jnp.concatenate([rows[:MAIN], rest, last], axis=1).astype(BF16)
    y_copies = [remote(slots.at[c, x, y], slots.at[c, x, y], y_send.at[k], y_recv.at[k], dev_y(k)) for k in range(1, NY)]
    for copy in y_copies:
        copy.start()
    o_copy = remote(own_hbm, own.at[c], o_send, o_recv, dev_c)
    o_copy.start()
    for group in z_copies[1:]:
        for copy in group:
            copy.start()

    for copy in locals_in:
        copy.wait()
    for k in ORDER:
        there = lax.rem(z + NZ - k, NZ)
        remote(mask_hbm, masks.at[there], m_send.at[k], m_recv.at[k], dev_z(k)).wait_recv()
    spread = jnp.where(iota((96, WIDTH), 0) == z * 8 + (iota((96, WIDTH), 1) >> 6), 1.0, 0.0).astype(BF16)
    entries = jnp.concatenate([masks[a] for a in range(NZ)] + [jnp.zeros((4, 96), I32)], axis=0).astype(F32).astype(BF16)
    keep[...] = jnp.dot(entries, spread, preferred_element_type=F32)

    remote(own_hbm, own.at[1 - c], o_send, o_recv, dev_c).wait_recv()
    target = z * 64 + iota((32, 96), 0) * 2 + c
    q = iota((96, 192), 1)
    t = iota((96, 192), 0)
    for j in range(CHUNKS):
        for par in range(2):
            picked = jnp.zeros((32, 192), F32)
            for core in range(2):
                qq = q - 96 * core
                wanted = (qq >> 3) * 8 + 2 * (j * (CW // LANES) + (qq & 7)) + par
                perm = jnp.where((t == wanted) & ((qq & 7) < CW // LANES) & (qq >= 0) & (qq < 96), 1.0, 0.0).astype(BF16)
                hit = jnp.where(own[core] == target, 1.0, 0.0).astype(BF16)
                picked = picked + jnp.dot(hit, perm, preferred_element_type=F32)
            hits[j, pl.ds(par * 32, 32), :] = picked.astype(BF16)

    def from_y(k):
        there = lax.rem(y + NY - k, NY)
        return remote(slots.at[c, x, there], slots.at[c, x, there], y_send.at[k], y_recv.at[k], dev_y(k))

    for k in range(1, NY):
        from_y(k).wait_recv()
    x_copies = [remote(slots.at[c, x], slots.at[c, x], x_send.at[k], x_recv.at[k], dev_x(k)) for k in (2, 1, 3)]
    for copy in x_copies:
        copy.start()

    def between(k, core):
        there = lax.rem(x + NX - k, NX)
        return remote(slots.at[core, there], slots.at[core, there], c_send.at[k], c_recv.at[k], dev_c)

    row = iota((288, 256), 0)
    col = iota((288, 256), 1)
    yy = jnp.zeros_like(row)
    for step in range(1, NY):
        yy = yy + (row >= 36 * step).astype(I32)
    row = row - 36 * yy
    cc = (row >= SHARD).astype(I32)
    row = row - SHARD * cc
    first_rows = jnp.where((row < MAIN) & (col == cc * 128 + yy * MAIN + row), 1.0, 0.0).astype(BF16)
    last_rows = jnp.where((row >= MAIN) & (col == cc * 16 + yy * 2 + row - MAIN), 1.0, 0.0).astype(BF16)[:, :32]
    row = iota((256, 256), 0)
    col = iota((256, 256), 1)
    slot = (row & 31) >> 1
    regroup = jnp.where(col == slot * MAIN + 2 * (row >> 5) + (row & 1), 1.0, 0.0).astype(BF16)

    def spread_rows(k):
        there = lax.rem(x + NX - k, NX)
        rest = [slots[:, there, :, :, pl.ds(NAUX + i * LANES, LANES)].reshape(256, LANES) for i in range(2)]
        pieces = jnp.dot(regroup, rest[0], preferred_element_type=F32).astype(BF16)
        piece = jnp.dot(regroup[:32], rest[1], preferred_element_type=F32).astype(BF16)
        ends = jnp.concatenate([pieces[32 * i : 32 * (i + 1)] for i in range(8)] + [piece], axis=1)
        for i in range(3):
            cols = pl.ds(i * 384, 384)
            main = slots[:, there, :, :, cols].reshape(256, 384)
            both = jnp.dot(first_rows, main, preferred_element_type=F32)
            both = both + jnp.dot(last_rows, ends[:, i * 384 : (i + 1) * 384], preferred_element_type=F32)
            dense[pl.ds(pl.multiple_of(there * 288, 32), 288), cols] = both.astype(BF16)

    c_copies = [between(k, c) for k in range(NX)]
    c_copies[0].start()
    for k, before in ((1, 0), (3, 1), (2, 3)):
        there = lax.rem(x + NX - k, NX)
        remote(slots.at[c, there], slots.at[c, there], x_send.at[k], x_recv.at[k], dev_x(k)).wait_recv()
        c_copies[k].start()
        between(before, 1 - c).wait_recv()
        spread_rows(before)
    between(2, 1 - c).wait_recv()
    spread_rows(2)

    def chunk(j):
        for k in (0,) + ORDER:
            there = lax.rem(z + NZ - k, NZ)
            if k:
                remote(columns(there, j), got.at[j, there], z_send.at[j, k], z_recv.at[j, k], dev_z(k)).wait_recv()
            got[j, there] = got[j, there] * keep[pl.ds(there, 1), pl.ds(j * CW, CW)].astype(BF16)
        block = got[j].reshape(NAUX, CW)
        acc = jnp.zeros((1, CW), F32)
        for i in range(NAUX // QB):
            image = jnp.dot(dense[pl.ds(i * QB, QB), :], block, preferred_element_type=F32)
            acc = acc + jnp.sum(block[i * QB : (i + 1) * QB].astype(F32) * image, axis=0, keepdims=True)
        pieces = [acc[:, i * LANES : (i + 1) * LANES] for i in range(CW // LANES)]
        terms[j] = jnp.concatenate(pieces + [jnp.zeros((8 - len(pieces), LANES), F32)], axis=0)
        copies = [
            remote(terms.at[j], heard.at[j, c * NZ + z], t_send.at[j, int(flip), k], t_recv.at[j], dev_zc(k, flip))
            for k in ORDER + (0,) for flip in (False, True) if k or flip
        ]
        for copy in copies:
            copy.start()
        heard[j, c * NZ + z] = terms[j]
        return copies

    def owned(j):
        others = heard.at[j, pl.ds(0, 2 * NZ - 1)]
        pltpu.make_async_copy(others, others, t_recv.at[j]).wait()
        value = heard[j].reshape(192, LANES)
        first = value.astype(BF16)
        value = value - first.astype(F32)
        second = value.astype(BF16)
        third = (value - second.astype(F32)).astype(BF16)
        sums = [jnp.dot(hits[j], v, preferred_element_type=F32) for v in (third, second, first)]
        both = sums[0] + sums[1] + sums[2]
        return both[:32, :64] + both[32:, 64:]

    t_copies = [chunk(0)]
    total = None
    for j in range(1, CHUNKS):
        t_copies.append(chunk(j))
        mine = owned(j - 1)
        total = mine if total is None else total + mine
    mine = owned(CHUNKS - 1)
    total = mine if total is None else total + mine

    total = jnp.concatenate([total, jnp.zeros((32, 64), F32)], axis=1)
    for i in range(NX * NY):
        part[i] = total[i : i + 1]
    p_copies = [
        remote(part.at[place_at(k)], rows_in.at[place], p_send.at[i], p_recv, dev_xy(k)) for i, k in enumerate(AROUND)
    ]
    for copy in p_copies:
        copy.start()
    rows_in[place] = part[place]
    others = rows_in.at[pl.ds(0, NX * NY - 1)]
    pltpu.make_async_copy(others, others, p_recv).wait()
    out_ref[...] = jnp.sum(rows_in[...], axis=0)[:, :64]

    for group in [y_copies, x_copies, c_copies, [o_copy], m_copies, p_copies] + z_copies + t_copies:
        for copy in group:
            copy.wait_send()


def body(integrals, tile_mask, metric, owners):
    any_spec = pl.BlockSpec(memory_space=pl.ANY)
    dma = pltpu.SemaphoreType.DMA
    return pl.pallas_call(
        kernel,
        out_shape=jax.ShapeDtypeStruct((1, 64), F32),
        in_specs=[any_spec] * 4,
        out_specs=pl.BlockSpec(memory_space=pltpu.VMEM),
        scratch_shapes=[
            pltpu.VMEM((CHUNKS, NZ, AUXD, CW), BF16),
            pltpu.VMEM((NZ, 1, 96), I32),
            pltpu.VMEM((16, WIDTH), F32),
            pltpu.VMEM((SHARD, NAUX), BF16),
            pltpu.VMEM((2, 1, 96), I32),
            pltpu.VMEM((2, NX, NY, MAIN, PACKED), BF16),
            pltpu.VMEM((NAUX, NAUX), BF16),
            pltpu.VMEM((CHUNKS, 64, 192), BF16),
            pltpu.VMEM((CHUNKS, 8, LANES), F32),
            pltpu.VMEM((CHUNKS, 2 * NZ, 8, LANES), F32),
            pltpu.VMEM((NX * NY, 1, LANES), F32),
            pltpu.VMEM((NX * NY, 1, LANES), F32),
            dma((3 + CHUNKS,)),
            dma((CHUNKS, NZ)), dma((CHUNKS, NZ)),
            dma((NZ,)), dma((NZ,)),
            dma, dma,
            dma((NY,)), dma((NY,)),
            dma((NX,)), dma((NX,)),
            dma((NX,)), dma((NX,)),
            dma((CHUNKS, 2, NZ)), dma((CHUNKS,)),
            dma((NX * NY,)), dma,
        ],
        compiler_params=pltpu.CompilerParams(collective_id=0, has_side_effects=True),
    )(integrals, tile_mask, metric, owners.reshape(1, -1))


def solution(mesh):
    return jax.shard_map(
        body,
        mesh=mesh,
        in_specs=(P("aux", "pair"), P("aux", "pair"), P("pair", None), P("pair")),
        out_specs=P(("aux", "pair"), None),
        check_vma=False,
    )
```

time: 291 us -> 78.5 us (0.27)
  blocking collectives: 182 us -> 0 us
  Pallas kernels: 0 us -> 77.2 us
  waiting for transfers between devices: 76.9 us -> 0 us
  between operations: 13.5 us -> 0.01 us
  local copies, waits for them, and re-layouts: 10.6 us -> 1.19 us
  matrix products: 7.12 us -> 0 us
    unnamed x1 -> x0, blocking collectives: 110 us -> none
    pallas_call x0 -> x1, Pallas kernels: none -> 77.2 us  [body(): pl.pallas_call(kernel, out_shape=jax.ShapeDtypeStruct((1, 64), F32), in_s...]
    all_gather x2 -> x0, waiting for transfers between devices: 76.1 us -> none  [the longest x1 53.7 us: body(): values = lax.all_gather(weights, ('aux', 'pair'), axis=0, tiled=True)]
    all_to_all x1 -> x0, blocking collectives: 72.1 us -> none  [body(): lax.all_to_all(blocks, 'aux', split_axis=1, concat_axis=0, tiled=True)]
    dot_general x2 -> x0, matrix products: 7.12 us -> none  [the longest x1 3.59 us: body(): jnp.dot(lax.all_gather(metric, 'pair', axis=0, tiled=True), flat, preferr...]
    unnamed x6 -> x1, local copies, waits for them, and re-layouts: 5.94 us -> 1.19 us
    reshape x2 -> x0, local copies, waits for them, and re-layouts: 3.42 us -> none  [the longest x1 2.74 us: body(): flat = moved.reshape(moved.shape[0], per_group * TILE)]
  transfers between devices with their start and end apart: 2 -> 0, of which waited for: 2 -> 0; matrix products, arithmetic and copies ran while one was open for 2% -> 0% of each run, Pallas kernels for 0% -> 0%
where the time goes in v2:
time: 78.5 us; the launch traced here: 78.4 us
  Pallas kernels  77.2 us (98%)
  local copies, waits for them, and re-layouts  1.19 us (2%)
    pallas_call x1, Pallas kernels, body(): pl.pallas_call(kernel, out_shape=jax.ShapeDtypeStruct((1, 64), F32), in_s...  77.2 us

profile of v2, /device:TPU:1, one launch (start us, length us, event | category | flops | bytes accessed | tf_op | source)
XLA Modules:
  0.0 78.4 jit_solution(8009519025551938879)
XLA Ops:
  0.0 77.2 %shard_map.46 = f32[1,64]{1,0:T(1,128)} custom-call(bf16[96,6144]{1,0:T(8,128)(2,1)} %x_hbm.1, s32[1,96]{1,0:T(1,128)} %mask_hbm.1, bf16[18,1152]{1,0:T(8,128)(2,1)} %met_hbm.1, s32[1,96]{1,0:T(1,128)} %bitcast.1), custom_call_target="tpu_custom_call" | custom-call | tf_op jit(solution)/shard_map/pallas_call | solution.py:254
  77.2 1.2 %copy.6 = f32[1,64]{1,0:T(1,128)} copy(f32[1,64]{1,0:T(1,128)} %shard_map.46) | data formatting | bytes 512

commit v3 on v2

--- a/solution.py
+++ b/solution.py
@@ -17,7 +17,7 @@
 SHARD = 18
 MAIN = 16
 PACKED = NAUX + 2 * LANES
-QB = 192
+QB = 576
 ORDER = (6, 5, 7, 4, 8, 3, 9, 2, 10, 1, 11)
 AROUND = sorted(
     [(i, j) for i in range(NX) for j in range(NY) if i or j], key=lambda k: -min(k[0], NX - k[0]) - min(k[1], NY - k[1])
@@ -36,36 +36,38 @@
 ):
     z = lax.axis_index("aux")
     pair = lax.axis_index("pair")
-    c = lax.rem(pair, 2)
-    y = lax.rem(pair // 2, NY)
-    x = pair // (2 * NY)
-    place = x * NY + y
+    c = pair & 1
+    y = (pair >> 1) & (NY - 1)
+    x = pair >> 4
+    place = pair >> 1
+
+    ahead = [z] + [jnp.where(z + k >= NZ, z + k - NZ, z + k) for k in range(1, NZ)]
 
     def at_z(k):
-        return lax.rem(z + k, NZ)
+        return ahead[k]
 
     def at_y(k):
-        return lax.rem(y + k, NY)
+        return (y + k) & (NY - 1)
 
     def dev_z(k):
         return {"aux": at_z(k)}
 
     def dev_zc(k, flip):
-        return {"aux": at_z(k), "pair": place * 2 + (1 - c if flip else c)}
+        return {"aux": at_z(k), "pair": pair ^ 1 if flip else pair}
 
     def dev_y(k):
         return {"pair": (x * NY + at_y(k)) * 2 + c}
 
     def place_at(k):
-        return lax.rem(x + k[0], NX) * NY + lax.rem(y + k[1], NY)
+        return ((x + k[0]) & (NX - 1)) * NY + ((y + k[1]) & (NY - 1))
 
     def dev_xy(k):
         return {"pair": place_at(k) * 2 + c}
 
     def dev_x(k):
-        return {"pair": (lax.rem(x + k, NX) * NY + y) * 2 + c}
-
-    dev_c = {"pair": (x * NY + y) * 2 + (1 - c)}
+        return {"pair": (((x + k) & (NX - 1)) * NY + y) * 2 + c}
+
+    dev_c = {"pair": pair ^ 1}
 
     def remote(s, d, ss, rs, dev):
         return pltpu.make_async_remote_copy(src_ref=s, dst_ref=d, send_sem=ss, recv_sem=rs, device_id=dev, device_id_type=MESH)
@@ -85,35 +87,34 @@
     ] + [pltpu.make_async_copy(columns(z, j), got.at[j, z], in_sem.at[3 + j]) for j in range(CHUNKS)]
     for copy in locals_in:
         copy.start()
-    pl.semaphore_wait(barrier, len(peers))
-
-    z_copies = [
-        [remote(columns(at_z(k), j), got.at[j, z], z_send.at[j, k], z_recv.at[j, k], dev_z(k)) for k in ORDER]
-        for j in range(CHUNKS)
-    ]
-    m_copies = [remote(mask_hbm, masks.at[z], m_send.at[k], m_recv.at[k], dev_z(k)) for k in ORDER]
-    for copy in m_copies + z_copies[0]:
-        copy.start()
-
     met_in.wait()
     rows = met[...].astype(F32)
     tail = rows[MAIN:SHARD]
     rest = jnp.concatenate([tail[:, i * LANES : (i + 1) * LANES] for i in range(8)], axis=0)
     last = jnp.concatenate([tail[:, 8 * LANES :], jnp.zeros((MAIN - 2, LANES), F32)], axis=0)
     slots[c, x, y] = jnp.concatenate([rows[:MAIN], rest, last], axis=1).astype(BF16)
+    pl.semaphore_wait(barrier, len(peers))
+
+    z_copies = [
+        [remote(columns(at_z(k), j), got.at[j, z], z_send.at[j, k], z_recv.at[j, k], dev_z(k)) for k in ORDER]
+        for j in range(CHUNKS)
+    ]
+    m_copies = [remote(mask_hbm, masks.at[z], m_send.at[k], m_recv.at[k], dev_z(k)) for k in ORDER]
     y_copies = [remote(slots.at[c, x, y], slots.at[c, x, y], y_send.at[k], y_recv.at[k], dev_y(k)) for k in range(1, NY)]
     for copy in y_copies:
         copy.start()
     o_copy = remote(own_hbm, own.at[c], o_send, o_recv, dev_c)
     o_copy.start()
-    for group in z_copies[1:]:
-        for copy in group:
-            copy.start()
+    for copy in m_copies:
+        copy.start()
+    for group, ks in ((0, ORDER[:7]), (1, ORDER[:7]), (0, ORDER[7:]), (1, ORDER[7:])):
+        for k in ks:
+            z_copies[group][ORDER.index(k)].start()
 
     for copy in locals_in:
         copy.wait()
     for k in ORDER:
-        there = lax.rem(z + NZ - k, NZ)
+        there = at_z((NZ - k) % NZ)
         remote(mask_hbm, masks.at[there], m_send.at[k], m_recv.at[k], dev_z(k)).wait_recv()
     spread = jnp.where(iota((96, WIDTH), 0) == z * 8 + (iota((96, WIDTH), 1) >> 6), 1.0, 0.0).astype(BF16)
     entries = jnp.concatenate([masks[a] for a in range(NZ)] + [jnp.zeros((4, 96), I32)], axis=0).astype(F32).astype(BF16)
@@ -135,7 +136,7 @@
             hits[j, pl.ds(par * 32, 32), :] = picked.astype(BF16)
 
     def from_y(k):
-        there = lax.rem(y + NY - k, NY)
+        there = ((y - k) & (NY - 1))
         return remote(slots.at[c, x, there], slots.at[c, x, there], y_send.at[k], y_recv.at[k], dev_y(k))
 
     for k in range(1, NY):
@@ -145,7 +146,7 @@
         copy.start()
 
     def between(k, core):
-        there = lax.rem(x + NX - k, NX)
+        there = ((x - k) & (NX - 1))
         return remote(slots.at[core, there], slots.at[core, there], c_send.at[k], c_recv.at[k], dev_c)
 
     row = iota((288, 256), 0)
@@ -164,7 +165,7 @@
     regroup = jnp.where(col == slot * MAIN + 2 * (row >> 5) + (row & 1), 1.0, 0.0).astype(BF16)
 
     def spread_rows(k):
-        there = lax.rem(x + NX - k, NX)
+        there = ((x - k) & (NX - 1))
         rest = [slots[:, there, :, :, pl.ds(NAUX + i * LANES, LANES)].reshape(256, LANES) for i in range(2)]
         pieces = jnp.dot(regroup, rest[0], preferred_element_type=F32).astype(BF16)
         piece = jnp.dot(regroup[:32], rest[1], preferred_element_type=F32).astype(BF16)
@@ -179,7 +180,7 @@
     c_copies = [between(k, c) for k in range(NX)]
     c_copies[0].start()
     for k, before in ((1, 0), (3, 1), (2, 3)):
-        there = lax.rem(x + NX - k, NX)
+        there = ((x - k) & (NX - 1))
         remote(slots.at[c, there], slots.at[c, there], x_send.at[k], x_recv.at[k], dev_x(k)).wait_recv()
         c_copies[k].start()
         between(before, 1 - c).wait_recv()
@@ -189,7 +190,7 @@
 
     def chunk(j):
         for k in (0,) + ORDER:
-            there = lax.rem(z + NZ - k, NZ)
+            there = at_z((NZ - k) % NZ)
             if k:
                 remote(columns(there, j), got.at[j, there], z_send.at[j, k], z_recv.at[j, k], dev_z(k)).wait_recv()
             got[j, there] = got[j, there] * keep[pl.ds(there, 1), pl.ds(j * CW, CW)].astype(BF16)
@@ -219,7 +220,7 @@
         third = (value - second.astype(F32)).astype(BF16)
         sums = [jnp.dot(hits[j], v, preferred_element_type=F32) for v in (third, second, first)]
         both = sums[0] + sums[1] + sums[2]
-        return both[:32, :64] + both[32:, 64:]
+        return jnp.where(iota((32, LANES), 1) < 64, both[:32], both[32:])
 
     t_copies = [chunk(0)]
     total = None
@@ -227,10 +228,12 @@
         t_copies.append(chunk(j))
         mine = owned(j - 1)
         total = mine if total is None else total + mine
+    for group in [y_copies, x_copies, c_copies, [o_copy], m_copies] + z_copies + t_copies:
+        for copy in group:
+            copy.wait_send()
     mine = owned(CHUNKS - 1)
     total = mine if total is None else total + mine
 
-    total = jnp.concatenate([total, jnp.zeros((32, 64), F32)], axis=1)
     for i in range(NX * NY):
         part[i] = total[i : i + 1]
     p_copies = [
@@ -239,13 +242,12 @@
     for copy in p_copies:
         copy.start()
     rows_in[place] = part[place]
+    for copy in p_copies:
+        copy.wait_send()
     others = rows_in.at[pl.ds(0, NX * NY - 1)]
     pltpu.make_async_copy(others, others, p_recv).wait()
-    out_ref[...] = jnp.sum(rows_in[...], axis=0)[:, :64]
-
-    for group in [y_copies, x_copies, c_copies, [o_copy], m_copies, p_copies] + z_copies + t_copies:
-        for copy in group:
-            copy.wait_send()
+    both = jnp.sum(rows_in[...], axis=0)
+    out_ref[...] = both[:, :64] + both[:, 64:]
 
 
 def body(integrals, tile_mask, metric, owners):

time: 78.5 us -> 78.1 us (level)
  no operation moved by 1% of the time
where the time goes in v3:
time: 78.1 us; the launch traced here: 77.9 us
  Pallas kernels  76.7 us (98%)
  local copies, waits for them, and re-layouts  1.19 us (2%)
    pallas_call x1, Pallas kernels, body(): pl.pallas_call(kernel, out_shape=jax.ShapeDtypeStruct((1, 64), F32), in_s...  76.7 us

profile of v3, /device:TPU:1, one launch (start us, length us, event | category | flops | bytes accessed | tf_op | source)
XLA Modules:
  0.0 77.9 jit_solution(17069296482172346597)
XLA Ops:
  0.0 76.7 %shard_map.46 = f32[1,64]{1,0:T(1,128)} custom-call(bf16[96,6144]{1,0:T(8,128)(2,1)} %x_hbm.1, s32[1,96]{1,0:T(1,128)} %mask_hbm.1, bf16[18,1152]{1,0:T(8,128)(2,1)} %met_hbm.1, s32[1,96]{1,0:T(1,128)} %bitcast.1), custom_call_target="tpu_custom_call" | custom-call | tf_op jit(solution)/shard_map/pallas_call | solution.py:256
  76.7 1.2 %copy.6 = f32[1,64]{1,0:T(1,128)} copy(f32[1,64]{1,0:T(1,128)} %shard_map.46) | data formatting | bytes 512

commit v4 on v3

--- a/solution.py
+++ b/solution.py
@@ -78,7 +78,7 @@
     met_in = pltpu.make_async_copy(met_hbm, met, in_sem.at[0])
     met_in.start()
     barrier = pltpu.get_barrier_semaphore()
-    peers = [dev_zc(k, False) for k in ORDER] + [dev_xy(k) for k in AROUND] + [dev_zc(k, True) for k in ORDER + (0,)]
+    peers = [dev_zc(k, False) for k in ORDER] + [dev_xy(k) for k in AROUND if 0 in k] + [dev_zc(0, True)]
     for peer in peers:
         pl.semaphore_signal(barrier, inc=1, device_id=peer, device_id_type=MESH)
     locals_in = [

time: 78.1 us -> 77.6 us (level)
  no operation moved by 1% of the time
where the time goes in v4:
time: 77.6 us; the launch traced here: 77.5 us
  Pallas kernels  76.3 us (98%)
  local copies, waits for them, and re-layouts  1.19 us (2%)
    pallas_call x1, Pallas kernels, body(): pl.pallas_call(kernel, out_shape=jax.ShapeDtypeStruct((1, 64), F32), in_s...  76.3 us

profile of v4, /device:TPU:1, one launch (start us, length us, event | category | flops | bytes accessed | tf_op | source)
XLA Modules:
  0.0 77.5 jit_solution(8080599741358415974)
XLA Ops:
  0.0 76.3 %shard_map.46 = f32[1,64]{1,0:T(1,128)} custom-call(bf16[96,6144]{1,0:T(8,128)(2,1)} %x_hbm.1, s32[1,96]{1,0:T(1,128)} %mask_hbm.1, bf16[18,1152]{1,0:T(8,128)(2,1)} %met_hbm.1, s32[1,96]{1,0:T(1,128)} %bitcast.1), custom_call_target="tpu_custom_call" | custom-call | tf_op jit(solution)/shard_map/pallas_call | solution.py:256
  76.3 1.2 %copy.6 = f32[1,64]{1,0:T(1,128)} copy(f32[1,64]{1,0:T(1,128)} %shard_map.46) | data formatting | bytes 512

commit v5 on v4

--- a/solution.py
+++ b/solution.py
@@ -87,27 +87,29 @@
     ] + [pltpu.make_async_copy(columns(z, j), got.at[j, z], in_sem.at[3 + j]) for j in range(CHUNKS)]
     for copy in locals_in:
         copy.start()
+    pl.semaphore_wait(barrier, len(peers))
+
+    z_copies = [
+        [remote(columns(at_z(k), j), got.at[j, z], z_send.at[j, k], z_recv.at[j, k], dev_z(k)) for k in ORDER]
+        for j in range(CHUNKS)
+    ]
+    m_copies = [remote(mask_hbm, masks.at[z], m_send.at[k], m_recv.at[k], dev_z(k)) for k in ORDER]
+    for copy in m_copies:
+        copy.start()
+    for copy in z_copies[0][:2]:
+        copy.start()
     met_in.wait()
     rows = met[...].astype(F32)
     tail = rows[MAIN:SHARD]
     rest = jnp.concatenate([tail[:, i * LANES : (i + 1) * LANES] for i in range(8)], axis=0)
     last = jnp.concatenate([tail[:, 8 * LANES :], jnp.zeros((MAIN - 2, LANES), F32)], axis=0)
     slots[c, x, y] = jnp.concatenate([rows[:MAIN], rest, last], axis=1).astype(BF16)
-    pl.semaphore_wait(barrier, len(peers))
-
-    z_copies = [
-        [remote(columns(at_z(k), j), got.at[j, z], z_send.at[j, k], z_recv.at[j, k], dev_z(k)) for k in ORDER]
-        for j in range(CHUNKS)
-    ]
-    m_copies = [remote(mask_hbm, masks.at[z], m_send.at[k], m_recv.at[k], dev_z(k)) for k in ORDER]
     y_copies = [remote(slots.at[c, x, y], slots.at[c, x, y], y_send.at[k], y_recv.at[k], dev_y(k)) for k in range(1, NY)]
     for copy in y_copies:
         copy.start()
     o_copy = remote(own_hbm, own.at[c], o_send, o_recv, dev_c)
     o_copy.start()
-    for copy in m_copies:
-        copy.start()
-    for group, ks in ((0, ORDER[:7]), (1, ORDER[:7]), (0, ORDER[7:]), (1, ORDER[7:])):
+    for group, ks in ((0, ORDER[2:7]), (1, ORDER[:7]), (0, ORDER[7:]), (1, ORDER[7:])):
         for k in ks:
             z_copies[group][ORDER.index(k)].start()
 

time: 77.6 us -> 77.6 us (level)
  no operation moved by 1% of the time
where the time goes in v5:
time: 77.6 us; the launch traced here: 77.5 us
  Pallas kernels  76.3 us (98%)
  local copies, waits for them, and re-layouts  1.19 us (2%)
    pallas_call x1, Pallas kernels, body(): pl.pallas_call(kernel, out_shape=jax.ShapeDtypeStruct((1, 64), F32), in_s...  76.3 us

profile of v5, /device:TPU:1, one launch (start us, length us, event | category | flops | bytes accessed | tf_op | source)
XLA Modules:
  0.0 77.5 jit_solution(15821248059854708115)
XLA Ops:
  0.0 76.3 %shard_map.46 = f32[1,64]{1,0:T(1,128)} custom-call(bf16[96,6144]{1,0:T(8,128)(2,1)} %x_hbm.1, s32[1,96]{1,0:T(1,128)} %mask_hbm.1, bf16[18,1152]{1,0:T(8,128)(2,1)} %met_hbm.1, s32[1,96]{1,0:T(1,128)} %bitcast.1), custom_call_target="tpu_custom_call" | custom-call | tf_op jit(solution)/shard_map/pallas_call | solution.py:258
  76.3 1.2 %copy.6 = f32[1,64]{1,0:T(1,128)} copy(f32[1,64]{1,0:T(1,128)} %shard_map.46) | data formatting | bytes 512
